TPU v7x, 512 devices: a whole 4x4x16 slice. The times are simulated.
512 devices in a mesh: group: 8 (over z_lo), member: 64 (over x, y, z_hi, core).
Axes of the slice: x: 4, y: 4, z: 16 (z_hi: 2, z_lo: 8; z = z_hi * 8 + z_lo), core: 2. Of those that a mesh axis runs over, the one named last changes fastest.
Arguments:
- embeddings: bfloat16 [262144, 1024], P(('group', 'member')), may hold values from -6 to 6
- assign: int32 [262144], P(('group', 'member')), may hold values from 0 to 255, as said below
- cluster_list: int32 [512, 64], P(('group', 'member')), may hold values from 0 to 255, as said below
- owner_map: int32 [8, 256], P('group'), may hold values from 0 to 255, as said below
- old_centroids: float32 [2048, 1024], P(('group', 'member')), may hold values from -16 to 16
Outputs:
- centroids: bfloat16 [2048, 1024], P(('group', 'member'))
- block_max: float32 [262144, 512], P(('group', 'member'))
Inputs may be any that keep to these rules, and one draw needn't show every extreme that they name: Each row of owner_map is a permutation; the centroid at position p of group g is row g * 256 + p of old_centroids and centroids. `cluster_list`: each device lists 64 distinct clusters of its group's slab. Of the 4 clusters whose positions p share p // 4, a device lists at most 2, and every device lists exactly 2 of some such set. `assign`: A cluster number within the slab of the row's group.
All inputs are finite; a program needn't handle non-finite values.
Results may differ from a plain program's by a relative error of at most 0.0023.
Values may be sent and summed in bfloat16 or wider, within the bound.
A program may use at most 64 MiB of HBM per device.

v0:
```python
import math

import jax
import jax.numpy as jnp
from jax import lax
from jax.sharding import PartitionSpec as P


def shards(embeddings, assign, cluster_list, owner_map, old_centroids):
    per_owner = old_centroids.shape[0]
    slab_rows = owner_map.shape[1]
    width = embeddings.shape[1]
    listed_ids = cluster_list[0]
    owner_row = owner_map[0]
    lookup = listed_ids[:, None] == jnp.arange(slab_rows, dtype=jnp.int32)[None, :]
    listed_pos = jnp.sum(jnp.where(lookup, owner_row[None, :], 0), axis=1)
    matched = assign[:, None] == listed_ids[None, :]
    row_target = jnp.sum(jnp.where(matched, listed_pos[None, :] + 1, 0), axis=1) - 1
    one_hot = (row_target[None, :] == jnp.arange(slab_rows, dtype=jnp.int32)[:, None]).astype(
        jnp.bfloat16
    )
    partial_value = jnp.dot(one_hot, embeddings, preferred_element_type=jnp.float32)
    tallies = jnp.sum(one_hot.astype(jnp.float32), axis=1)
    cluster_sums, counts = (
        lax.psum_scatter(partial_value, "member", scatter_dimension=0, tiled=True),
        lax.psum_scatter(tallies, "member", scatter_dimension=0, tiled=True),
    )
    updated = (cluster_sums + old_centroids) / (counts + 1.0)[:, None]
    centroids = (
        updated * lax.rsqrt(jnp.mean(updated * updated, axis=1, keepdims=True) + 1e-05)
    ).astype(jnp.bfloat16)
    inverse_root = 1.0 / math.sqrt(width)
    whole_slab = lax.all_gather(centroids, "member", axis=0, tiled=True)
    shard_rows = lax.all_gather(whole_slab, "group", axis=0, tiled=True)
    similarity = (
        lax.dot_general(
            embeddings, shard_rows, (((1,), (1,)), ((), ())), preferred_element_type=jnp.float32
        )
        * inverse_root
    )
    blocks = jnp.max(
        similarity.reshape(similarity.shape[0], shard_rows.shape[0] // per_owner, per_owner), axis=2
    )
    return (centroids, blocks)


def solution(mesh):
    in_specs = (
        P(("group", "member"), None),
        P(("group", "member")),
        P(("group", "member"), None),
        P("group", None),
        P(("group", "member"), None),
    )
    out_specs = (P(("group", "member"), None), P(("group", "member"), None))
    return jax.shard_map(shards, mesh=mesh, in_specs=in_specs, out_specs=out_specs, check_vma=False)
```

profile of v0, /device:TPU:1, one launch (start us, length us, event | category | flops | bytes accessed | tf_op | source)
XLA Modules:
  0.0 1374.8 jit_solution(14540987311990371259)
XLA Ops:
  7.2 0.0 copy-start
  7.2 0.0 all-reduce.4.cloned.1.call-start
  7.2 0.9 select_reduce_fusion.1
  8.2 0.8 select_reduce_fusion
  9.0 0.0 copy-done
  9.0 1.4 fusion.1
  10.4 0.0 all-reduce.4.cloned.1.call-update
  10.4 0.0 all-gather.3.cloned.1.call-start
  10.5 1.3 dynamic-slice
  12.4 0.1 convert_reduce_fusion
  12.5 284.2 %all-reduce.1 = f32[256]{0:T(256)S(1)} all-reduce(f32[256]{0:T(256)S(1)} %convert_reduce_fusion), channel_id=3, replica_groups=mesh['group'=8,'member'=64] {'member'}, use_global_device_ids=true, to_apply=%region_4.5.clone | all-reduce | flops 256 | bytes 2048
  296.7 0.1 dynamic-slice_add_fusion.1
  296.8 797.9 %all-reduce.4.cloned.1.call-done = f32[256,1024]{1,0:T(8,128)} async-done(((f32[256,1024]{1,0:T(8,128)}), f32[256,1024]{1,0:T(8,128)}) %all-reduce.4.cloned.1.call-update) | async-done | bytes 1048592
  1094.7 1.0 multiply_reduce_fusion
  1095.6 0.1 fusion.8
  1095.7 161.9 %all-gather = bf16[64,4,1024]{2,1,0:T(4,128)(2,1)S(1)} all-gather(bf16[1,4,1024]{2,1,0:T(4,128)(2,1)S(1)} %fusion.8), channel_id=1, replica_groups=mesh['group'=8,'member'=64] {'member'}, dimensions={0}, use_global_device_ids=true | all-gather | bytes 532480 | tf_op jit(solution)/shard_map/all_gather | solution.py:33
  1257.6 0.9 reshape.27
  1258.6 0.0 all-gather.3.cloned.1.call-update
  1258.6 0.7 multiply_convert_fusion
  1259.3 91.1 %all-gather.3.cloned.1.call-done = bf16[2048,1024]{1,0:T(8,128)(2,1)} async-done(((bf16[256,1024]{1,0:T(8,128)(2,1)}), bf16[2048,1024]{1,0:T(8,128)(2,1)}) %all-gather.3.cloned.1.call-update) | async-done | bytes 4194320 | tf_op jit(solution)/shard_map/all_gather | solution.py:34
  1350.3 6.5 multiply_bitcast_fusion
  1356.8 5.2 reshape.25
  1362.0 4.7 reduce_max.9
  1366.7 1.3 copy.8
  (3 shorter events, 0.0 us)
Async XLA Ops:
  7.2 1.8 copy-start
  7.2 1087.5 %all-reduce.4.cloned.1.call-start = ((), (), s32[]{:S(2)}) async-start(), calls=%async_computation.1 | async-start | bytes 2097152
  10.4 1339.9 %all-gather.3.cloned.1.call-start = ((), (), s32[]{:S(2)}) async-start(), calls=%async_computation | async-start | bytes 4718592 | tf_op jit(solution)/shard_map/all_gather | solution.py:34
Sparse Core Ops, SparseCore 0:
  11.5 1083.1 all-reduce.3
  1258.7 91.5 all-gather.2
where the time goes:
time: 1380 us; the launch traced here: 1370 us
  waiting for transfers between devices  889 us (64%)
  blocking collectives  446 us (32%)
  between operations  14.7 us (1%)
    unnamed x3, waiting for transfers between devices  798 us
    unnamed x1, blocking collectives  284 us
    all_gather x1, blocking collectives, shards(): whole_slab = lax.all_gather(centroids, 'member', axis=0, tiled=True)  162 us
    all_gather x1, waiting for transfers between devices, shards(): shard_rows = lax.all_gather(whole_slab, 'group', axis=0, tiled=True)  91.1 us
  transfers between devices with their start and end apart: 2, of which 2 were waited for; matrix products, arithmetic and copies ran while one was open for 0% of the time, Pallas kernels for 0%

commit v1 on v0

v1 whole, which is shorter than its diff:
```python
import math

import jax
import jax.numpy as jnp
from jax import lax
from jax.experimental import pallas as pl
from jax.experimental.pallas import tpu as pltpu
from jax.sharding import PartitionSpec as P

F32, BF16, I32 = jnp.float32, jnp.bfloat16, jnp.int32
MSG = 640
OFFSETS = (0, 1, -1, 2, -2, 3, -3, 4)


def iota(shape, dim):
    return lax.broadcasted_iota(I32, shape, dim)


def split3(v):
    hi = v.astype(BF16)
    rest = v - hi.astype(F32)
    mid = rest.astype(BF16)
    low = (rest - mid.astype(F32)).astype(BF16)
    return hi, mid, low


def column_of(row, n):
    eye = iota((n, n), 0) == iota((n, n), 1)
    return jnp.sum(jnp.where(eye, row, 0), axis=1, keepdims=True)


def row_of(col, n):
    eye = iota((n, n), 0) == iota((n, n), 1)
    return jnp.sum(jnp.where(eye, col, 0), axis=0, keepdims=True)


def slot_rows(list_row, pos_row):
    lists = list_row.shape[1]
    listed = jnp.max(
        jnp.where(list_row == iota((256, lists), 0), 1, 0), axis=1, keepdims=True
    )
    pos_col = column_of(pos_row, 256)
    key = jnp.where(listed > 0, pos_col, -8)
    rank = jnp.sum(
        jnp.where(((key >> 2) == (pos_row >> 2)) & (key < pos_row), 1, 0), axis=0, keepdims=True
    )
    listed_row = row_of(listed, 256)
    chip = pos_row >> 4
    core = (pos_row >> 2) & 1
    high = (pos_row >> 3) & 1
    turned = ((chip & 3) << 2) | (chip >> 2)
    target = core * 16 + jnp.where(core == 0, chip, turned)
    slot = jnp.where(listed_row > 0, target * 4 + high * 2 + rank + 1, 0)
    return slot, high * 4 + (pos_row & 3)


def kernel(
    emb, assign, listing, owner, old, cent_out, out,
    perm, send, recv, zsend, zrecv, raw, slab,
    a2a_send, a2a_recv, zx_send, zx_recv, ag_send, z_recv, step_recv,
):
    g = lax.axis_index("group")
    m = lax.axis_index("member")
    x, y, zh, c = m // 16, (m // 4) % 4, (m // 2) % 2, m % 2
    z = zh * 8 + g
    a = jnp.where(c == 0, y, x)
    b = jnp.where(c == 0, x, y)
    me = c * 16 + b * 4 + a

    def at_plane(core, bb, aa):
        xx = jnp.where(core == 0, bb, aa)
        yy = jnp.where(core == 0, aa, bb)
        return {"member": xx * 16 + yy * 4 + zh * 2 + core}

    def at_z(zz):
        zz = (zz + 16) % 16
        return {"group": zz % 8, "member": x * 16 + y * 4 + (zz // 8) * 2 + c}

    def plane_peer(i):
        t = (me + i) % 32
        return t, at_plane(t // 16, (t // 4) % 4, t % 4)

    barrier = pltpu.get_barrier_semaphore()

    def greet(i, carry):
        pl.semaphore_signal(barrier, inc=1, device_id=plane_peer(i)[1])
        return carry

    lax.fori_loop(1, 32, greet, 0)
    for d in (1, -1, 2, -2, 3, -3, 4, -4, 8):
        pl.semaphore_signal(barrier, inc=1, device_id=at_z(z + d))

    slot_row, line_row = slot_rows(listing[...], owner[...])
    slot_col = column_of(slot_row, 256)
    row_slot = jnp.sum(
        jnp.where(assign[...] == iota((256, 512), 0), slot_col, 0), axis=0, keepdims=True
    )
    index = iota((256, 1), 0)
    half = (index >> 2) & 1
    wanted = ((index >> 3) << 2 | (index & 3)) + 1
    member_of = row_slot == wanted
    member_f = jnp.where(member_of, 1.0, 0.0)
    count = jnp.sum(member_f, axis=1, keepdims=True)
    member_b = member_f.astype(BF16)
    line = jnp.sum(jnp.where(slot_row == wanted, line_row + 1, 0), axis=1, keepdims=True) - 1
    lane = iota((256, 128), 1)
    mark = jnp.where(((lane & 7) == line) & ((lane >> 3) == half), 1.0, 0.0)
    send[:, 512:] = jnp.where(lane < 16, mark, count)
    for col in range(0, 512, 256):
        low = jnp.dot(member_b, emb[:, col:col + 256], preferred_element_type=F32)
        high = jnp.dot(member_b, emb[:, 512 + col:512 + col + 256], preferred_element_type=F32)
        send[:, col:col + 256] = jnp.where(half == 0, low, high)

    pl.semaphore_wait(barrier, 40)

    def give(i, carry):
        t, peer = plane_peer(i)
        pltpu.make_async_remote_copy(
            src_ref=send.at[pl.ds(pl.multiple_of(t * 8, 8), 8)],
            dst_ref=recv.at[pl.ds(pl.multiple_of(me * 8, 8), 8)],
            send_sem=a2a_send,
            recv_sem=a2a_recv,
            device_id=peer,
        ).start()
        return carry

    lax.fori_loop(1, 32, give, 0)
    mine = pl.ds(pl.multiple_of(me * 8, 8), 8)
    recv[mine, :] = send[mine, :]

    k = iota((1, 512), 1)
    kc, kb, ka = k >> 8, (k >> 6) & 3, (k >> 4) & 3
    block = jnp.where(kc == 0, kb * 4 + ka, ka * 4 + kb) * 4 + ((k >> 2) & 1) * 2 + kc
    goal = ((k >> 3) & 1) * 256 + (k & 3) * 64 + block
    perm[...] = jnp.where(goal == iota((512, 512), 0), 1.0, 0.0).astype(BF16)
    out[...] = jnp.zeros_like(out)

    def all_but_one(src, dst, ssem, rsem, peer):
        return pltpu.make_async_remote_copy(
            src_ref=src.at[pl.ds(0, 248)], dst_ref=dst.at[pl.ds(0, 248)],
            send_sem=ssem, recv_sem=rsem, device_id=peer,
        )

    whole = all_but_one(send, recv, a2a_send, a2a_recv, plane_peer(1)[1])
    whole.wait_recv()
    marks = jnp.where(lane < 16, recv[:, 512:], 0.0).astype(BF16)
    total = None
    for part in split3(recv[...]):
        term = lax.dot_general(
            marks, part, (((0,), (0,)), ((), ())), preferred_element_type=F32
        )[:16]
        total = term if total is None else total + term
    line16 = iota((16, 1), 0) & 7
    prior = jnp.zeros((16, 512), F32)
    upper = iota((16, 1), 0) >= 8
    for j in range(4):
        rows = jnp.where(upper, old[j:j + 1, 512:], old[j:j + 1, :512])
        prior = prior + jnp.where(line16 == zh * 4 + j, rows, 0.0)
    zsend[:, :512] = total[:, :512] + prior
    zsend[:, 512:] = total[:, 512:]
    across = pltpu.make_async_remote_copy(
        src_ref=zsend, dst_ref=zrecv, send_sem=zx_send, recv_sem=zx_recv, device_id=at_z(z + 8)
    )
    across.start()
    across.wait_recv()
    tally = zsend[:, 512 + 16:512 + 17] + zrecv[:, 512 + 16:512 + 17]
    updated = (zsend[:, :512] + zrecv[:, :512]) / (tally + 1.0)
    squares = jnp.sum(updated * updated, axis=1, keepdims=True)
    mean = (squares[:8] + squares[8:]) * (1.0 / 1024)
    scale = lax.rsqrt(mean + 1e-05)
    cent = updated * jnp.concatenate([scale, scale], axis=0)
    for h in range(2):
        part = cent[8 * h:8 * h + 8]
        cent_out[:, 512 * h:512 * h + 512] = jnp.where(zh == 0, part[:4], part[4:]).astype(BF16)

    def at_row(gg, bb, aa):
        return pl.multiple_of((((c * 8 + gg) * 4 + bb) * 4 + aa) * 16, 16)

    raw[pl.ds(at_row(g, b, a), 16), :] = cent.astype(BF16)

    def copy(row, rows, sem, peer, cols=None):
        ref = raw.at[pl.ds(row, rows)] if cols is None else raw.at[pl.ds(row, rows), cols]
        return pltpu.make_async_remote_copy(
            src_ref=ref, dst_ref=ref, send_sem=ag_send, recv_sem=sem, device_id=peer
        )

    for n in range(1, 8):
        copy(at_row(g, b, a), 16, z_recv.at[n], at_z(z - OFFSETS[n])).start()

    left, right = (a + 3) % 4, (a + 1) % 4
    down, up = (b + 3) % 4, (b + 1) % 4
    far_a, far_b = (a + 2) % 4, (b + 2) % 4
    to_left, to_right = at_plane(c, b, left), at_plane(c, b, right)
    to_down, to_up = at_plane(c, down, a), at_plane(c, up, a)
    sibling = {"member": m + 1 - 2 * c}
    lo, hi = pl.ds(0, 256), pl.ds(256, 256)

    def group_of(n):
        offset = jnp.where(n % 2 == 1, (n + 1) // 2, -(n // 2))
        return (z + offset + 16) % 8

    def stage_z(n):
        gg = group_of(n)

        @pl.when(n > 0)
        def _():
            copy(at_row(gg, b, a), 16, z_recv.at[n], sibling).wait_recv()

        copy(at_row(gg, b, a), 16, step_recv.at[0, n], to_right).start()
        copy(at_row(gg, b, a), 16, step_recv.at[1, n], to_left).start()

    def stage_a(n):
        gg = group_of(n)
        copy(at_row(gg, b, left), 16, step_recv.at[0, n], to_right).wait_recv()
        copy(at_row(gg, b, left), 16, step_recv.at[2, n], to_right, lo).start()
        copy(at_row(gg, b, right), 16, step_recv.at[1, n], to_left).wait_recv()
        copy(at_row(gg, b, right), 16, step_recv.at[3, n], to_left, hi).start()

    def stage_a_far(n):
        gg = group_of(n)
        copy(at_row(gg, b, far_a), 16, step_recv.at[2, n], to_right, lo).wait_recv()
        copy(at_row(gg, b, far_a), 16, step_recv.at[3, n], to_left, hi).wait_recv()
        copy(at_row(gg, b, 0), 64, step_recv.at[4, n], to_up).start()
        copy(at_row(gg, b, 0), 64, step_recv.at[5, n], to_down).start()

    def stage_b(n):
        gg = group_of(n)
        copy(at_row(gg, down, 0), 64, step_recv.at[4, n], to_up).wait_recv()
        copy(at_row(gg, down, 0), 32, step_recv.at[6, n], to_up).start()
        copy(at_row(gg, up, 0), 64, step_recv.at[5, n], to_down).wait_recv()
        copy(at_row(gg, up, 2), 32, step_recv.at[7, n], to_down).start()

    def stage_b_far(n):
        gg = group_of(n)
        copy(at_row(gg, far_b, 0), 32, step_recv.at[6, n], to_up).wait_recv()
        copy(at_row(gg, far_b, 2), 32, step_recv.at[7, n], to_down).wait_recv()
        copy(at_row(gg, 0, 0), 256, step_recv.at[8, n], sibling).start()

    def stage_dot(n):
        gg = group_of(n)
        theirs = pl.multiple_of(((1 - c) * 8 + gg) * 256, 256)
        pltpu.make_async_remote_copy(
            src_ref=raw.at[pl.ds(theirs, 256)], dst_ref=raw.at[pl.ds(theirs, 256)],
            send_sem=ag_send, recv_sem=step_recv.at[8, n], device_id=sibling,
        ).wait_recv()
        first = raw[pl.ds(pl.multiple_of(gg * 256, 256), 256), :]
        second = raw[pl.ds(pl.multiple_of((8 + gg) * 256, 256), 256), :]
        for h in range(2):
            rows = slice(256 * h, 256 * h + 256)
            turned = jnp.dot(perm[rows, :256], first, preferred_element_type=F32)
            turned = turned + jnp.dot(perm[rows, 256:], second, preferred_element_type=F32)
            slab[:, 512 * h:512 * h + 512] = turned.astype(BF16)
        lanes = pl.ds(pl.multiple_of((gg // 2) * 128, 128), 128)
        for r in range(0, 512, 256):
            sim = lax.dot_general(
                emb[r:r + 256, :], slab[...], (((1,), (1,)), ((), ())), preferred_element_type=F32
            )
            best = jnp.maximum(sim[:, :128], sim[:, 128:])
            best = jnp.maximum(best, pltpu.roll(best, 64, 1)) * (1.0 / math.sqrt(1024))
            keep = (iota((256, 128), 1) >> 6) == gg % 2
            out[r:r + 256, lanes] = jnp.where(keep, best, out[r:r + 256, lanes])

    stages = (stage_z, stage_a, stage_a_far, stage_b, stage_b_far, stage_dot)

    def tick(i, carry):
        for lag, stage in enumerate(stages):
            n = i - lag

            @pl.when((n >= 0) & (n < 8))
            def _(stage=stage, n=n):
                stage(n)

        return carry

    lax.fori_loop(0, 8 + len(stages) - 1, tick, 0)

    whole.wait_send()
    across.wait_send()
    sent = 7 * 16 + 8 * (32 + 16) + 8 * (128 + 64) + 8 * 256
    pltpu.make_async_remote_copy(
        src_ref=raw.at[pl.ds(0, sent)], dst_ref=raw.at[pl.ds(0, sent)],
        send_sem=ag_send, recv_sem=z_recv.at[0], device_id=sibling,
    ).wait_send()


def shards(embeddings, assign, cluster_list, owner_map, old_centroids):
    vmem = pl.BlockSpec(memory_space=pltpu.VMEM)
    return pl.pallas_call(
        kernel,
        out_shape=(
            jax.ShapeDtypeStruct((4, 1024), BF16),
            jax.ShapeDtypeStruct((512, 512), F32),
        ),
        in_specs=[vmem] * 5,
        out_specs=(vmem, vmem),
        scratch_shapes=[
            pltpu.VMEM((512, 512), BF16),
            pltpu.VMEM((256, MSG), F32),
            pltpu.VMEM((256, MSG), F32),
            pltpu.VMEM((16, MSG), F32),
            pltpu.VMEM((16, MSG), F32),
            pltpu.VMEM((4096, 512), BF16),
            pltpu.VMEM((256, 1024), BF16),
            pltpu.SemaphoreType.DMA,
            pltpu.SemaphoreType.DMA,
            pltpu.SemaphoreType.DMA,
            pltpu.SemaphoreType.DMA,
            pltpu.SemaphoreType.DMA,
            pltpu.SemaphoreType.DMA((8,)),
            pltpu.SemaphoreType.DMA((9, 8)),
        ],
        compiler_params=pltpu.CompilerParams(
            collective_id=0, has_side_effects=True, vmem_limit_bytes=48 * 1024 * 1024
        ),
    )(embeddings, assign.reshape(1, -1), cluster_list, owner_map, old_centroids)


def solution(mesh):
    rows = P(("group", "member"), None)
    return jax.shard_map(
        shards,
        mesh=mesh,
        in_specs=(rows, P(("group", "member")), rows, P("group", None), rows),
        out_specs=(rows, rows),
        check_vma=False,
    )
```

time: 1380 us -> 76.9 us (0.06)
  waiting for transfers between devices: 889 us -> 0 us
  blocking collectives: 446 us -> 0 us
  Pallas kernels: 0 us -> 71.2 us
  between operations: 14.7 us -> 0.66 us
    unnamed x3 -> x0, waiting for transfers between devices: 798 us -> none
    unnamed x1 -> x0, blocking collectives: 284 us -> none
    all_gather x1 -> x0, blocking collectives: 162 us -> none  [shards(): whole_slab = lax.all_gather(centroids, 'member', axis=0, tiled=True)]
    all_gather x1 -> x0, waiting for transfers between devices: 91.1 us -> none  [shards(): shard_rows = lax.all_gather(whole_slab, 'group', axis=0, tiled=True)]
    pallas_call x0 -> x1, Pallas kernels: none -> 71.2 us  [shards(): pl.pallas_call(kernel, out_shape=(jax.ShapeDtypeStruct((4, 1024), BF16),...]
  transfers between devices with their start and end apart: 2 -> 0, of which waited for: 2 -> 0; matrix products, arithmetic and copies ran while one was open for 0% -> 0% of each run, Pallas kernels for 0% -> 0%
where the time goes in v1:
time: 76.9 us; the launch traced here: 76.7 us
  Pallas kernels  71.2 us (93%)
  local copies, waits for them, and re-layouts  4.86 us (6%)
    pallas_call x1, Pallas kernels, shards(): pl.pallas_call(kernel, out_shape=(jax.ShapeDtypeStruct((4, 1024), BF16),...  71.2 us
    unnamed x12, local copies, waits for them, and re-layouts  4.86 us

profile of v1, /device:TPU:1, one launch (start us, length us, event | category | flops | bytes accessed | tf_op | source)
XLA Modules:
  0.0 76.7 jit_solution(6247013573409830158)
XLA Ops:
  0.6 0.0 copy-start.3
  0.6 0.0 copy-start.4
  0.7 0.7 copy-done.3
  1.3 0.0 copy-done.4
  1.3 0.0 copy-start
  1.3 1.2 %copy-done = bf16[512,1024]{1,0:T(8,128)(2,1)S(1)} copy-done((bf16[512,1024]{1,0:T(8,128)(2,1)S(1)}, bf16[512,1024]{1,0:T(8,128)(2,1)}, u32[]{:S(2)}) %copy-start) | copy-done | bytes 1048600
  2.5 0.0 copy-start.1
  2.5 0.7 copy-done.1
  3.3 0.0 copy-start.2
  3.3 0.7 copy-done.2
  3.9 71.2 %shard_map.68 = (bf16[4,1024]{1,0:T(4,128)(2,1)S(1)}, f32[512,512]{1,0:T(8,128)S(1)}) custom-call(bf16[512,1024]{1,0:T(8,128)(2,1)S(1)} %copy-done, s32[1,512]{1,0:T(1,128)S(1)} %bitcast.1, s32[1,64]{1,0:T(1,128)S(1)} %copy-done.4, s32[1,256]{1,0:T(1,128)S(1)} %copy-done.3, f32[4,1024]{1,0:T(4,128)S(1)} %copy-done.1), custom_call_target="tpu_custom_call" | custom-call | tf_op jit(solution)/shard_map/pallas_call | solution.py:288
  75.1 0.6 copy.9
  75.7 1.0 %copy.10 = f32[512,512]{1,0:T(8,128)} copy(f32[512,512]{1,0:T(8,128)S(1)} %get-tuple-element.5) | data formatting | bytes 2097152
Async XLA Ops:
  0.6 0.7 copy-start.3
  0.6 0.7 copy-start.4
  1.3 1.2 %copy-start = (bf16[512,1024]{1,0:T(8,128)(2,1)S(1)}, bf16[512,1024]{1,0:T(8,128)(2,1)}, u32[]{:S(2)}) copy-start(bf16[512,1024]{1,0:T(8,128)(2,1)} %emb.1) | copy-start | bytes 3145732
  2.5 0.7 copy-start.1
  3.3 0.7 copy-start.2

commit v2 on v1

v2 whole, which is shorter than its diff:
```python
import math

import jax
import jax.numpy as jnp
from jax import lax
from jax.experimental import pallas as pl
from jax.experimental.pallas import tpu as pltpu
from jax.sharding import PartitionSpec as P

F32, BF16, I32 = jnp.float32, jnp.bfloat16, jnp.int32
MSG = 640
OFFSETS = (0, 1, -1, 2, -2, 3, -3, 4)
BATCHES = ((0, 1), (1, 3), (3, 5), (5, 7), (7, 8))


def iota(shape, dim):
    return lax.broadcasted_iota(I32, shape, dim)


def split3(v):
    hi = v.astype(BF16)
    rest = v - hi.astype(F32)
    mid = rest.astype(BF16)
    low = (rest - mid.astype(F32)).astype(BF16)
    return hi, mid, low


def column_of(row, n):
    eye = iota((n, n), 0) == iota((n, n), 1)
    return jnp.sum(jnp.where(eye, row, 0), axis=1, keepdims=True)


def row_of(col, n):
    eye = iota((n, n), 0) == iota((n, n), 1)
    return jnp.sum(jnp.where(eye, col, 0), axis=0, keepdims=True)


def slot_rows(list_row, pos_row):
    lists = list_row.shape[1]
    listed = jnp.max(
        jnp.where(list_row == iota((256, lists), 0), 1, 0), axis=1, keepdims=True
    )
    pos_col = column_of(pos_row, 256)
    key = jnp.where(listed > 0, pos_col, -8)
    rank = jnp.sum(
        jnp.where(((key >> 2) == (pos_row >> 2)) & (key < pos_row), 1, 0), axis=0, keepdims=True
    )
    listed_row = row_of(listed, 256)
    chip = pos_row >> 4
    core = (pos_row >> 2) & 1
    high = (pos_row >> 3) & 1
    turned = ((chip & 3) << 2) | (chip >> 2)
    target = core * 16 + jnp.where(core == 0, chip, turned)
    slot = jnp.where(listed_row > 0, target * 4 + high * 2 + rank + 1, 0)
    return slot, high * 4 + (pos_row & 3)


def kernel(
    emb_hbm, assign_hbm, listing_hbm, owner_hbm, old_hbm, cent_out, out,
    emb, assign, listing, owner, old,
    perm, send, recv, zsend, zrecv, raw, slab,
    load_sem, a2a_send, a2a_recv, zx_send, zx_recv, ag_send, z_recv, a_recv, b_recv, core_recv,
):
    g = lax.axis_index("group")
    m = lax.axis_index("member")
    x, y, zh, c = m // 16, (m // 4) % 4, (m // 2) % 2, m % 2
    z = zh * 8 + g
    a = jnp.where(c == 0, y, x)
    b = jnp.where(c == 0, x, y)
    me = c * 16 + b * 4 + a

    def at_plane(core, bb, aa):
        xx = jnp.where(core == 0, bb, aa)
        yy = jnp.where(core == 0, aa, bb)
        return {"member": xx * 16 + yy * 4 + zh * 2 + core}

    def at_z(zz):
        zz = (zz + 16) % 16
        return {"group": zz % 8, "member": x * 16 + y * 4 + (zz // 8) * 2 + c}

    def plane_peer(i):
        t = (me + i) % 32
        return t, at_plane(t // 16, (t // 4) % 4, t % 4)

    barrier = pltpu.get_barrier_semaphore()

    def greet(i, carry):
        pl.semaphore_signal(barrier, inc=1, device_id=plane_peer(i)[1])
        return carry

    lax.fori_loop(1, 32, greet, 0)
    for d in (1, -1, 2, -2, 3, -3, 4, -4):
        pl.semaphore_signal(barrier, inc=1, device_id=at_z(z + d))

    loads = [
        pltpu.make_async_copy(src, dst, load_sem.at[i])
        for i, (src, dst) in enumerate(
            ((owner_hbm, owner), (listing_hbm, listing), (assign_hbm, assign), (emb_hbm, emb), (old_hbm, old))
        )
    ]
    for load in loads:
        load.start()
    loads[0].wait()
    loads[1].wait()

    slot_row, line_row = slot_rows(listing[...], owner[...])
    slot_col = column_of(slot_row, 256)
    loads[2].wait()
    row_slot = jnp.sum(
        jnp.where(assign[...] == iota((256, 512), 0), slot_col, 0), axis=0, keepdims=True
    )
    index = iota((256, 1), 0)
    half = (index >> 2) & 1
    wanted = ((index >> 3) << 2 | (index & 3)) + 1
    member_of = row_slot == wanted
    member_f = jnp.where(member_of, 1.0, 0.0)
    count = jnp.sum(member_f, axis=1, keepdims=True)
    member_b = member_f.astype(BF16)
    line = jnp.sum(jnp.where(slot_row == wanted, line_row + 1, 0), axis=1, keepdims=True) - 1
    lane = iota((256, 128), 1)
    mark = jnp.where(((lane & 7) == line) & ((lane >> 3) == half), 1.0, 0.0)
    send[:, 512:] = jnp.where(lane < 16, mark, count)
    loads[3].wait()
    for col in range(0, 512, 256):
        low = jnp.dot(member_b, emb[:, col:col + 256], preferred_element_type=F32)
        high = jnp.dot(member_b, emb[:, 512 + col:512 + col + 256], preferred_element_type=F32)
        send[:, col:col + 256] = jnp.where(half == 0, low, high)

    pl.semaphore_wait(barrier, 39)

    def give(i, carry):
        t, peer = plane_peer(i)
        pltpu.make_async_remote_copy(
            src_ref=send.at[pl.ds(pl.multiple_of(t * 8, 8), 8)],
            dst_ref=recv.at[pl.ds(pl.multiple_of(me * 8, 8), 8)],
            send_sem=a2a_send,
            recv_sem=a2a_recv,
            device_id=peer,
        ).start()
        return carry

    lax.fori_loop(1, 32, give, 0)
    mine = pl.ds(pl.multiple_of(me * 8, 8), 8)
    recv[mine, :] = send[mine, :]

    k = iota((1, 512), 1)
    kc, kb, ka = k >> 8, (k >> 6) & 3, (k >> 4) & 3
    block = jnp.where(kc == 0, kb * 4 + ka, ka * 4 + kb) * 4 + ((k >> 2) & 1) * 2 + kc
    goal = ((k >> 3) & 1) * 256 + (k & 3) * 64 + block
    perm[...] = jnp.where(goal == iota((512, 512), 0), 1.0, 0.0).astype(BF16)
    out[...] = jnp.zeros_like(out)

    def all_but_one(src, dst, ssem, rsem, peer):
        return pltpu.make_async_remote_copy(
            src_ref=src.at[pl.ds(0, 248)], dst_ref=dst.at[pl.ds(0, 248)],
            send_sem=ssem, recv_sem=rsem, device_id=peer,
        )

    whole = all_but_one(send, recv, a2a_send, a2a_recv, plane_peer(1)[1])
    whole.wait_recv()
    marks = jnp.where(lane < 16, recv[:, 512:], 0.0).astype(BF16)
    total = None
    for part in split3(recv[...]):
        term = lax.dot_general(
            marks, part, (((0,), (0,)), ((), ())), preferred_element_type=F32
        )[:16]
        total = term if total is None else total + term
    loads[4].wait()
    line16 = iota((16, 1), 0) & 7
    prior = jnp.zeros((16, 512), F32)
    upper = iota((16, 1), 0) >= 8
    for j in range(4):
        rows = jnp.where(upper, old[j:j + 1, 512:], old[j:j + 1, :512])
        prior = prior + jnp.where(line16 == zh * 4 + j, rows, 0.0)
    zsend[:, :512] = total[:, :512] + prior
    zsend[:, 512:] = total[:, 512:]
    across = [
        pltpu.make_async_remote_copy(
            src_ref=zsend, dst_ref=zrecv.at[i], send_sem=zx_send.at[i], recv_sem=zx_recv.at[i],
            device_id=at_z(z + d),
        )
        for i, d in enumerate((4, -4))
    ]
    for move in across:
        move.start()
    for move in across:
        move.wait_recv()
    tally = zrecv[0, :, 512 + 16:512 + 17] + zrecv[1, :, 512 + 16:512 + 17]
    updated = (zrecv[0, :, :512] + zrecv[1, :, :512]) / (tally + 1.0)
    squares = jnp.sum(updated * updated, axis=1, keepdims=True)
    mean = (squares[:8] + squares[8:]) * (1.0 / 1024)
    scale = lax.rsqrt(mean + 1e-05)
    raw[c, 0, b, a] = (updated * jnp.concatenate([scale, scale], axis=0)).astype(BF16)

    def copy(ref, sem, peer):
        return pltpu.make_async_remote_copy(
            src_ref=ref, dst_ref=ref, send_sem=ag_send, recv_sem=sem, device_id=peer
        )

    sibling = {"member": m + 1 - 2 * c}

    def z_piece(n):
        return pltpu.make_async_remote_copy(
            src_ref=raw.at[c, 0, b, a], dst_ref=raw.at[c, n, b, a],
            send_sem=ag_send, recv_sem=z_recv.at[n], device_id=at_z(z - OFFSETS[n]),
        )

    for n in range(1, 8):
        z_piece(n).start()

    def along_a(k, i, back):
        lo, hi = BATCHES[k]
        aa = (a + 4 - i) % 4 if back else a
        return copy(raw.at[c, lo:hi, b, aa], a_recv.at[k, i], at_plane(c, b, (a + i) % 4))

    def along_b(k, i, back):
        lo, hi = BATCHES[k]
        bb = (b + 4 - i) % 4 if back else b
        return copy(raw.at[c, lo:hi, bb], b_recv.at[k, i], at_plane(c, (b + i) % 4, a))

    def across_cores(k, core):
        lo, hi = BATCHES[k]
        return copy(raw.at[core, lo:hi], core_recv.at[k], sibling)

    def stage_z(k):
        for n in range(*BATCHES[k]):
            if n:
                z_piece(n).wait_recv()
        for i in (1, 3, 2):
            along_a(k, i, False).start()

    def stage_a(k):
        for i in (1, 3, 2):
            along_a(k, i, True).wait_recv()
        for i in (1, 3, 2):
            along_b(k, i, False).start()

    def stage_b(k):
        for i in (1, 3, 2):
            along_b(k, i, True).wait_recv()
        across_cores(k, c).start()

    def one_group(n, carry):
        offset = jnp.where(n % 2 == 1, (n + 1) // 2, -(n // 2))
        gg = (z + offset + 20) % 8
        first = raw[0, n].reshape(256, 512)
        second = raw[1, n].reshape(256, 512)
        for h in range(2):
            rows = slice(256 * h, 256 * h + 256)
            turned = jnp.dot(perm[rows, :256], first, preferred_element_type=F32)
            turned = turned + jnp.dot(perm[rows, 256:], second, preferred_element_type=F32)
            slab[:, 512 * h:512 * h + 512] = turned.astype(BF16)
        lanes = pl.ds(pl.multiple_of((gg // 2) * 128, 128), 128)
        for r in range(0, 512, 256):
            sim = lax.dot_general(
                emb[r:r + 256, :], slab[...], (((1,), (1,)), ((), ())), preferred_element_type=F32
            )
            best = jnp.maximum(sim[:, :128], sim[:, 128:])
            best = jnp.maximum(best, pltpu.roll(best, 64, 1)) * (1.0 / math.sqrt(1024))
            keep = (iota((256, 128), 1) >> 6) == gg % 2
            out[r:r + 256, lanes] = jnp.where(keep, best, out[r:r + 256, lanes])
        return carry

    def stage_dot(k):
        across_cores(k, 1 - c).wait_recv()
        lax.fori_loop(*BATCHES[k], one_group, 0)

    stage_z(0)
    stage_z(1)
    stage_z(2)
    stage_a(0)
    stage_z(3)
    stage_z(4)
    own = raw[c, 7, b, a].astype(F32)
    for h in range(2):
        part = own[8 * h:8 * h + 8]
        cent_out[:, 512 * h:512 * h + 512] = jnp.where(zh == 0, part[:4], part[4:]).astype(BF16)
    stage_a(1)
    stage_a(2)
    stage_b(0)
    stage_a(3)
    stage_a(4)
    stage_dot(0)
    stage_b(1)
    stage_b(2)
    stage_dot(1)
    stage_b(3)
    stage_dot(2)
    stage_b(4)
    stage_dot(3)
    stage_dot(4)

    whole.wait_send()
    for move in across:
        move.wait_send()
    sent = raw.reshape(4096, 512).at[pl.ds(0, 255 * 16)]
    copy(sent, z_recv.at[0], sibling).wait_send()


def shards(embeddings, assign, cluster_list, owner_map, old_centroids):
    vmem = pl.BlockSpec(memory_space=pltpu.VMEM)
    return pl.pallas_call(
        kernel,
        out_shape=(
            jax.ShapeDtypeStruct((4, 1024), BF16),
            jax.ShapeDtypeStruct((512, 512), F32),
        ),
        in_specs=[pl.BlockSpec(memory_space=pl.ANY)] * 5,
        out_specs=(vmem, vmem),
        scratch_shapes=[
            pltpu.VMEM((512, 1024), BF16),
            pltpu.VMEM((1, 512), I32),
            pltpu.VMEM((1, 64), I32),
            pltpu.VMEM((1, 256), I32),
            pltpu.VMEM((4, 1024), F32),
            pltpu.VMEM((512, 512), BF16),
            pltpu.VMEM((256, MSG), F32),
            pltpu.VMEM((256, MSG), F32),
            pltpu.VMEM((16, MSG), F32),
            pltpu.VMEM((2, 16, MSG), F32),
            pltpu.VMEM((2, 8, 4, 4, 16, 512), BF16),
            pltpu.VMEM((256, 1024), BF16),
            pltpu.SemaphoreType.DMA((5,)),
            pltpu.SemaphoreType.DMA,
            pltpu.SemaphoreType.DMA,
            pltpu.SemaphoreType.DMA((2,)),
            pltpu.SemaphoreType.DMA((2,)),
            pltpu.SemaphoreType.DMA,
            pltpu.SemaphoreType.DMA((8,)),
            pltpu.SemaphoreType.DMA((5, 4)),
            pltpu.SemaphoreType.DMA((5, 4)),
            pltpu.SemaphoreType.DMA((5,)),
        ],
        compiler_params=pltpu.CompilerParams(
            collective_id=0, has_side_effects=True, vmem_limit_bytes=60 * 1024 * 1024
        ),
    )(embeddings, assign.reshape(1, -1), cluster_list, owner_map, old_centroids)


def solution(mesh):
    rows = P(("group", "member"), None)
    return jax.shard_map(
        shards,
        mesh=mesh,
        in_specs=(rows, P(("group", "member")), rows, P("group", None), rows),
        out_specs=(rows, rows),
        check_vma=False,
    )
```

time: 76.9 us -> 62.8 us (0.82)
  Pallas kernels: 71.2 us -> 58.4 us
  local copies, waits for them, and re-layouts: 4.86 us -> 3.56 us
    pallas_call x1, Pallas kernels: 71.2 us -> 58.4 us  [shards(): pl.pallas_call(kernel, out_shape=(jax.ShapeDtypeStruct((4, 1024), BF16),...]
    unnamed x12 -> x2, local copies, waits for them, and re-layouts: 4.86 us -> 3.56 us
where the time goes in v2:
time: 62.8 us; the launch traced here: 62.6 us
  Pallas kernels  58.4 us (93%)
  local copies, waits for them, and re-layouts  3.56 us (6%)
  between operations  0.64 us (1%)
    pallas_call x1, Pallas kernels, shards(): pl.pallas_call(kernel, out_shape=(jax.ShapeDtypeStruct((4, 1024), BF16),...  58.4 us
    unnamed x2, local copies, waits for them, and re-layouts  3.56 us

profile of v2, /device:TPU:1, one launch (start us, length us, event | category | flops | bytes accessed | tf_op | source)
XLA Modules:
  0.0 62.6 jit_solution(3967459973796976515)
XLA Ops:
  0.6 58.4 %shard_map.68 = (bf16[4,1024]{1,0:T(4,128)(2,1)}, f32[512,512]{1,0:T(8,128)}) custom-call(bf16[512,1024]{1,0:T(8,128)(2,1)} %emb_hbm.1, s32[1,512]{1,0:T(1,128)} %bitcast.1, s32[1,64]{1,0:T(1,128)} %listing_hbm.1, s32[1,256]{1,0:T(1,128)} %owner_hbm.1, f32[4,1024]{1,0:T(4,128)} %old_hbm.1), custom_call_target="tpu_custom_call" | custom-call | tf_op jit(solution)/shard_map/pallas_call | solution.py:302
  59.1 1.3 %copy.9 = bf16[4,1024]{1,0:T(4,128)(2,1)} copy(bf16[4,1024]{1,0:T(4,128)(2,1)} %get-tuple-element.4) | data formatting | bytes 16384
  60.4 2.3 %copy.10 = f32[512,512]{1,0:T(8,128)} copy(f32[512,512]{1,0:T(8,128)} %get-tuple-element.5) | data formatting | bytes 2097152

commit v3 on v2

--- a/solution.py
+++ b/solution.py
@@ -7,8 +7,9 @@
 from jax.experimental.pallas import tpu as pltpu
 from jax.sharding import PartitionSpec as P
 
-F32, BF16, I32 = jnp.float32, jnp.bfloat16, jnp.int32
-MSG = 640
+F32, BF16, I32, I16 = jnp.float32, jnp.bfloat16, jnp.int32, jnp.int16
+MSG = 384
+ZMSG = 640
 OFFSETS = (0, 1, -1, 2, -2, 3, -3, 4)
 BATCHES = ((0, 1), (1, 3), (3, 5), (5, 7), (7, 8))
 
@@ -17,12 +18,15 @@
     return lax.broadcasted_iota(I32, shape, dim)
 
 
-def split3(v):
-    hi = v.astype(BF16)
-    rest = v - hi.astype(F32)
-    mid = rest.astype(BF16)
-    low = (rest - mid.astype(F32)).astype(BF16)
-    return hi, mid, low
+def split2(v):
+    high = v.astype(BF16)
+    return high, (v - high.astype(F32)).astype(BF16)
+
+
+def quantise(v):
+    top = jnp.maximum(jnp.max(jnp.abs(v), axis=1, keepdims=True), 1e-30)
+    exponent = jnp.ceil(jnp.log2(top * (1.0 / 32000)))
+    return jnp.floor(v * jnp.exp2(-exponent) + 0.5).astype(I32).astype(I16), exponent
 
 
 def column_of(row, n):
@@ -79,8 +83,14 @@
         return {"group": zz % 8, "member": x * 16 + y * 4 + (zz // 8) * 2 + c}
 
     def plane_peer(i):
-        t = (me + i) % 32
-        return t, at_plane(t // 16, (t // 4) % 4, t % 4)
+        def step(j):
+            return jnp.where(j == 0, 2, jnp.where(j == 1, 1, jnp.where(j == 2, 3, 0)))
+
+        xx = (x + step(i // 8)) % 4
+        yy = (y + step((i // 2) % 4)) % 4
+        core = (c + i + 1) % 2
+        t = core * 16 + jnp.where(core == 0, xx * 4 + yy, yy * 4 + xx)
+        return t, {"member": xx * 16 + yy * 4 + zh * 2 + core}
 
     barrier = pltpu.get_barrier_semaphore()
 
@@ -88,7 +98,7 @@
         pl.semaphore_signal(barrier, inc=1, device_id=plane_peer(i)[1])
         return carry
 
-    lax.fori_loop(1, 32, greet, 0)
+    lax.fori_loop(0, 31, greet, 0)
     for d in (1, -1, 2, -2, 3, -3, 4, -4):
         pl.semaphore_signal(barrier, inc=1, device_id=at_z(z + d))
 
@@ -109,38 +119,39 @@
     row_slot = jnp.sum(
         jnp.where(assign[...] == iota((256, 512), 0), slot_col, 0), axis=0, keepdims=True
     )
-    index = iota((256, 1), 0)
-    half = (index >> 2) & 1
-    wanted = ((index >> 3) << 2 | (index & 3)) + 1
-    member_of = row_slot == wanted
-    member_f = jnp.where(member_of, 1.0, 0.0)
+    index = iota((512, 1), 0)
+    quarter = (index >> 2) & 3
+    wanted = ((index >> 4) << 2 | (index & 3)) + 1
+    member_f = jnp.where(row_slot == wanted, 1.0, 0.0)
     count = jnp.sum(member_f, axis=1, keepdims=True)
     member_b = member_f.astype(BF16)
     line = jnp.sum(jnp.where(slot_row == wanted, line_row + 1, 0), axis=1, keepdims=True) - 1
-    lane = iota((256, 128), 1)
-    mark = jnp.where(((lane & 7) == line) & ((lane >> 3) == half), 1.0, 0.0)
-    send[:, 512:] = jnp.where(lane < 16, mark, count)
+    lane = iota((512, 128), 1)
+    mark = jnp.where(((lane & 7) == line) & ((lane >> 3) == quarter), 1.0, 0.0)
     loads[3].wait()
-    for col in range(0, 512, 256):
-        low = jnp.dot(member_b, emb[:, col:col + 256], preferred_element_type=F32)
-        high = jnp.dot(member_b, emb[:, 512 + col:512 + col + 256], preferred_element_type=F32)
-        send[:, col:col + 256] = jnp.where(half == 0, low, high)
+    partial = jnp.zeros((512, 256), F32)
+    for k in range(4):
+        term = jnp.dot(member_b, emb[:, 256 * k:256 * k + 256], preferred_element_type=F32)
+        partial = jnp.where(quarter == k, term, partial)
+    send[:, :256], exponent = quantise(partial)
+    notes = jnp.where(lane < 32, mark, jnp.where(lane < 64, count, exponent))
+    send[:, 256:] = notes.astype(I32).astype(I16)
 
     pl.semaphore_wait(barrier, 39)
 
     def give(i, carry):
         t, peer = plane_peer(i)
         pltpu.make_async_remote_copy(
-            src_ref=send.at[pl.ds(pl.multiple_of(t * 8, 8), 8)],
-            dst_ref=recv.at[pl.ds(pl.multiple_of(me * 8, 8), 8)],
+            src_ref=send.at[pl.ds(pl.multiple_of(t * 16, 16), 16)],
+            dst_ref=recv.at[pl.ds(pl.multiple_of(me * 16, 16), 16)],
             send_sem=a2a_send,
             recv_sem=a2a_recv,
             device_id=peer,
         ).start()
         return carry
 
-    lax.fori_loop(1, 32, give, 0)
-    mine = pl.ds(pl.multiple_of(me * 8, 8), 8)
+    lax.fori_loop(0, 31, give, 0)
+    mine = pl.ds(pl.multiple_of(me * 16, 16), 16)
     recv[mine, :] = send[mine, :]
 
     k = iota((1, 512), 1)
@@ -152,28 +163,41 @@
 
     def all_but_one(src, dst, ssem, rsem, peer):
         return pltpu.make_async_remote_copy(
-            src_ref=src.at[pl.ds(0, 248)], dst_ref=dst.at[pl.ds(0, 248)],
+            src_ref=src.at[pl.ds(0, 496)], dst_ref=dst.at[pl.ds(0, 496)],
             send_sem=ssem, recv_sem=rsem, device_id=peer,
         )
 
-    whole = all_but_one(send, recv, a2a_send, a2a_recv, plane_peer(1)[1])
+    whole = all_but_one(send, recv, a2a_send, a2a_recv, plane_peer(0)[1])
     whole.wait_recv()
-    marks = jnp.where(lane < 16, recv[:, 512:], 0.0).astype(BF16)
-    total = None
-    for part in split3(recv[...]):
-        term = lax.dot_general(
-            marks, part, (((0,), (0,)), ((), ())), preferred_element_type=F32
-        )[:16]
-        total = term if total is None else total + term
+    notes = recv[:, 256:].astype(I32).astype(F32)
+    marks = jnp.where(lane < 32, notes, 0.0)
+    scaled = (marks * jnp.exp2(notes[:, 64:65])).astype(BF16)
+    marks = marks.astype(BF16)
+
+    def gathered(weights, values):
+        return lax.dot_general(
+            weights, values, (((0,), (0,)), ((), ())), preferred_element_type=F32
+        )[:32]
+
+    high, low = split2(recv[:, :256].astype(I32).astype(F32))
+    total = gathered(scaled, high) + gathered(scaled, low)
+    high, low = split2(notes)
+    tally = (gathered(marks, high) + gathered(marks, low))[:16, 32:33]
     loads[4].wait()
-    line16 = iota((16, 1), 0) & 7
-    prior = jnp.zeros((16, 512), F32)
-    upper = iota((16, 1), 0) >= 8
-    for j in range(4):
-        rows = jnp.where(upper, old[j:j + 1, 512:], old[j:j + 1, :512])
-        prior = prior + jnp.where(line16 == zh * 4 + j, rows, 0.0)
-    zsend[:, :512] = total[:, :512] + prior
-    zsend[:, 512:] = total[:, 512:]
+    line8 = iota((8, 1), 0)
+    parts = []
+    for k in range(4):
+        part = total[8 * k:8 * k + 8]
+        for j in range(4):
+            part = part + jnp.where(line8 == zh * 4 + j, old[j:j + 1, 256 * k:256 * k + 256], 0.0)
+        parts.append(part)
+    sums = jnp.concatenate(
+        [jnp.concatenate(parts[:2], axis=1), jnp.concatenate(parts[2:], axis=1)], axis=0
+    )
+    zsend[:, :512], exponent = quantise(sums)
+    notes = jnp.where(iota((16, 128), 1) < 64, tally, exponent)
+    zsend[:, 512:] = notes.astype(I32).astype(I16)
+
     across = [
         pltpu.make_async_remote_copy(
             src_ref=zsend, dst_ref=zrecv.at[i], send_sem=zx_send.at[i], recv_sem=zx_recv.at[i],
@@ -185,8 +209,13 @@
         move.start()
     for move in across:
         move.wait_recv()
-    tally = zrecv[0, :, 512 + 16:512 + 17] + zrecv[1, :, 512 + 16:512 + 17]
-    updated = (zrecv[0, :, :512] + zrecv[1, :, :512]) / (tally + 1.0)
+    sums = jnp.zeros((16, 512), F32)
+    tally = jnp.zeros((16, 1), F32)
+    for i in range(2):
+        notes = zrecv[i, :, 512:].astype(I32).astype(F32)
+        sums = sums + zrecv[i, :, :512].astype(I32).astype(F32) * jnp.exp2(notes[:, 64:65])
+        tally = tally + notes[:, :1]
+    updated = sums / (tally + 1.0)
     squares = jnp.sum(updated * updated, axis=1, keepdims=True)
     mean = (squares[:8] + squares[8:]) * (1.0 / 1024)
     scale = lax.rsqrt(mean + 1e-05)
@@ -205,7 +234,7 @@
             send_sem=ag_send, recv_sem=z_recv.at[n], device_id=at_z(z - OFFSETS[n]),
         )
 
-    for n in range(1, 8):
+    for n in (7, 5, 6, 3, 4, 1, 2):
         z_piece(n).start()
 
     def along_a(k, i, back):
@@ -226,13 +255,13 @@
         for n in range(*BATCHES[k]):
             if n:
                 z_piece(n).wait_recv()
-        for i in (1, 3, 2):
+        for i in (2, 1, 3):
             along_a(k, i, False).start()
 
     def stage_a(k):
         for i in (1, 3, 2):
             along_a(k, i, True).wait_recv()
-        for i in (1, 3, 2):
+        for i in (2, 1, 3):
             along_b(k, i, False).start()
 
     def stage_b(k):
@@ -302,8 +331,8 @@
     return pl.pallas_call(
         kernel,
         out_shape=(
-            jax.ShapeDtypeStruct((4, 1024), BF16),
-            jax.ShapeDtypeStruct((512, 512), F32),
+            pltpu.VMEM((4, 1024), BF16),
+            pltpu.VMEM((512, 512), F32),
         ),
         in_specs=[pl.BlockSpec(memory_space=pl.ANY)] * 5,
         out_specs=(vmem, vmem),
@@ -314,10 +343,10 @@
             pltpu.VMEM((1, 256), I32),
             pltpu.VMEM((4, 1024), F32),
             pltpu.VMEM((512, 512), BF16),
-            pltpu.VMEM((256, MSG), F32),
-            pltpu.VMEM((256, MSG), F32),
-            pltpu.VMEM((16, MSG), F32),
-            pltpu.VMEM((2, 16, MSG), F32),
+            pltpu.VMEM((512, MSG), I16),
+            pltpu.VMEM((512, MSG), I16),
+            pltpu.VMEM((16, ZMSG), I16),
+            pltpu.VMEM((2, 16, ZMSG), I16),
             pltpu.VMEM((2, 8, 4, 4, 16, 512), BF16),
             pltpu.VMEM((256, 1024), BF16),
             pltpu.SemaphoreType.DMA((5,)),

time: 62.8 us -> 55.6 us (0.89)
  Pallas kernels: 58.4 us -> 53.3 us
  local copies, waits for them, and re-layouts: 3.56 us -> 1.57 us
    pallas_call x1, Pallas kernels: 58.4 us -> 53.3 us  [shards(): pl.pallas_call(kernel, out_shape=(pltpu.VMEM((4, 1024), BF16), pltpu.VMEM...]
    unnamed x2, local copies, waits for them, and re-layouts: 3.56 us -> 1.57 us
where the time goes in v3:
time: 55.6 us; the launch traced here: 55.5 us
  Pallas kernels  53.3 us (96%)
  local copies, waits for them, and re-layouts  1.57 us (3%)
  between operations  0.64 us (1%)
    pallas_call x1, Pallas kernels, shards(): pl.pallas_call(kernel, out_shape=(pltpu.VMEM((4, 1024), BF16), pltpu.VMEM...  53.3 us
    unnamed x2, local copies, waits for them, and re-layouts  1.57 us

profile of v3, /device:TPU:1, one launch (start us, length us, event | category | flops | bytes accessed | tf_op | source)
XLA Modules:
  0.0 55.5 jit_solution(8503969062465409631)
XLA Ops:
  0.6 53.3 %shard_map.68 = (bf16[4,1024]{1,0:T(4,128)(2,1)S(1)}, f32[512,512]{1,0:T(8,128)S(1)}) custom-call(bf16[512,1024]{1,0:T(8,128)(2,1)} %emb_hbm.1, s32[1,512]{1,0:T(1,128)} %bitcast.1, s32[1,64]{1,0:T(1,128)} %listing_hbm.1, s32[1,256]{1,0:T(1,128)} %owner_hbm.1, f32[4,1024]{1,0:T(4,128)} %old_hbm.1), custom_call_target="tpu_custom_call" | custom-call | tf_op jit(solution)/shard_map/pallas_call | solution.py:331
  53.9 0.6 %copy.9 = bf16[4,1024]{1,0:T(4,128)(2,1)} copy(bf16[4,1024]{1,0:T(4,128)(2,1)S(1)} %get-tuple-element.2) | data formatting | bytes 16384
  54.5 1.0 %copy.10 = f32[512,512]{1,0:T(8,128)} copy(f32[512,512]{1,0:T(8,128)S(1)} %get-tuple-element.3) | data formatting | bytes 2097152

commit v4 on v3

--- a/solution.py
+++ b/solution.py
@@ -11,6 +11,7 @@
 MSG = 384
 ZMSG = 640
 OFFSETS = (0, 1, -1, 2, -2, 3, -3, 4)
+SIDE = {1: (0, -1, 3), 2: (0, 1, 1), 5: (3, -1, 3), 6: (4, 1, 1)}
 BATCHES = ((0, 1), (1, 3), (3, 5), (5, 7), (7, 8))
 
 
@@ -63,7 +64,7 @@
     emb_hbm, assign_hbm, listing_hbm, owner_hbm, old_hbm, cent_out, out,
     emb, assign, listing, owner, old,
     perm, send, recv, zsend, zrecv, raw, slab,
-    load_sem, a2a_send, a2a_recv, zx_send, zx_recv, ag_send, z_recv, a_recv, b_recv, core_recv,
+    load_sem, a2a_send, a2a_recv, zx_send, zx_recv, ag_send, z_recv, a_recv, b_recv, side_recv, core_recv,
 ):
     g = lax.axis_index("group")
     m = lax.axis_index("member")
@@ -234,7 +235,7 @@
             send_sem=ag_send, recv_sem=z_recv.at[n], device_id=at_z(z - OFFSETS[n]),
         )
 
-    for n in (7, 5, 6, 3, 4, 1, 2):
+    for n in (1, 2, 3, 4, 5, 6, 7):
         z_piece(n).start()
 
     def along_a(k, i, back):
@@ -244,12 +245,21 @@
 
     def along_b(k, i, back):
         lo, hi = BATCHES[k]
+        if lo % 4 == 1:
+            lo, hi = (lo + 1, hi) if i == 1 else (lo, hi - 1)
         bb = (b + 4 - i) % 4 if back else b
         return copy(raw.at[c, lo:hi, bb], b_recv.at[k, i], at_plane(c, (b + i) % 4, a))
 
-    def across_cores(k, core):
-        lo, hi = BATCHES[k]
-        return copy(raw.at[core, lo:hi], core_recv.at[k], sibling)
+    def from_z(n, j):
+        source, dz, near = SIDE[n]
+        chunk = (b + (2, near)[j]) % 4
+        return pltpu.make_async_remote_copy(
+            src_ref=raw.at[c, source, chunk], dst_ref=raw.at[c, n, chunk],
+            send_sem=ag_send, recv_sem=side_recv.at[n, j], device_id=at_z(z + dz),
+        )
+
+    def across_cores(n, core):
+        return copy(raw.at[core, n], core_recv.at[n], sibling)
 
     def stage_z(k):
         for n in range(*BATCHES[k]):
@@ -258,16 +268,28 @@
         for i in (2, 1, 3):
             along_a(k, i, False).start()
 
+    def peers_of(k):
+        return (1, 3) if BATCHES[k][0] % 4 == 1 else (2, 1, 3)
+
     def stage_a(k):
         for i in (1, 3, 2):
             along_a(k, i, True).wait_recv()
-        for i in (2, 1, 3):
+        for i in peers_of(k):
             along_b(k, i, False).start()
 
     def stage_b(k):
-        for i in (1, 3, 2):
+        for i in reversed(peers_of(k)):
             along_b(k, i, True).wait_recv()
-        across_cores(k, c).start()
+        for n in range(*BATCHES[k]):
+            for target in SIDE:
+                if SIDE[target][0] == n:
+                    from_z(target, 0).start()
+                    from_z(target, 1).start()
+        for n in range(*BATCHES[k]):
+            if n in SIDE:
+                from_z(n, 0).wait_recv()
+                from_z(n, 1).wait_recv()
+            across_cores(n, c).start()
 
     def one_group(n, carry):
         offset = jnp.where(n % 2 == 1, (n + 1) // 2, -(n // 2))
@@ -291,8 +313,11 @@
         return carry
 
     def stage_dot(k):
-        across_cores(k, 1 - c).wait_recv()
-        lax.fori_loop(*BATCHES[k], one_group, 0)
+        def piece(n, carry):
+            across_cores(n, 1 - c).wait_recv()
+            return one_group(n, carry)
+
+        lax.fori_loop(*BATCHES[k], piece, 0)
 
     stage_z(0)
     stage_z(1)
@@ -305,19 +330,19 @@
         part = own[8 * h:8 * h + 8]
         cent_out[:, 512 * h:512 * h + 512] = jnp.where(zh == 0, part[:4], part[4:]).astype(BF16)
     stage_a(1)
+    stage_b(0)
     stage_a(2)
-    stage_b(0)
     stage_a(3)
     stage_a(4)
     stage_dot(0)
     stage_b(1)
     stage_b(2)
     stage_dot(1)
+    stage_b(4)
+    stage_dot(2)
     stage_b(3)
-    stage_dot(2)
-    stage_b(4)
+    stage_dot(4)
     stage_dot(3)
-    stage_dot(4)
 
     whole.wait_send()
     for move in across:
@@ -358,7 +383,8 @@
             pltpu.SemaphoreType.DMA((8,)),
             pltpu.SemaphoreType.DMA((5, 4)),
             pltpu.SemaphoreType.DMA((5, 4)),
-            pltpu.SemaphoreType.DMA((5,)),
+            pltpu.SemaphoreType.DMA((8, 2)),
+            pltpu.SemaphoreType.DMA((8,)),
         ],
         compiler_params=pltpu.CompilerParams(
             collective_id=0, has_side_effects=True, vmem_limit_bytes=60 * 1024 * 1024

time: 55.6 us -> 53.9 us (0.969)
  Pallas kernels: 53.3 us -> 51.5 us
    pallas_call x1, Pallas kernels: 53.3 us -> 51.5 us  [shards(): pl.pallas_call(kernel, out_shape=(pltpu.VMEM((4, 1024), BF16), pltpu.VMEM...]
where the time goes in v4:
time: 53.9 us; the launch traced here: 53.7 us
  Pallas kernels  51.5 us (96%)
  local copies, waits for them, and re-layouts  1.57 us (3%)
  between operations  0.64 us (1%)
    pallas_call x1, Pallas kernels, shards(): pl.pallas_call(kernel, out_shape=(pltpu.VMEM((4, 1024), BF16), pltpu.VMEM...  51.5 us
    unnamed x2, local copies, waits for them, and re-layouts  1.57 us

profile of v4, /device:TPU:1, one launch (start us, length us, event | category | flops | bytes accessed | tf_op | source)
XLA Modules:
  0.0 53.7 jit_solution(12103558280768348207)
XLA Ops:
  0.6 51.5 %shard_map.68 = (bf16[4,1024]{1,0:T(4,128)(2,1)S(1)}, f32[512,512]{1,0:T(8,128)S(1)}) custom-call(bf16[512,1024]{1,0:T(8,128)(2,1)} %emb_hbm.1, s32[1,512]{1,0:T(1,128)} %bitcast.1, s32[1,64]{1,0:T(1,128)} %listing_hbm.1, s32[1,256]{1,0:T(1,128)} %owner_hbm.1, f32[4,1024]{1,0:T(4,128)} %old_hbm.1), custom_call_target="tpu_custom_call" | custom-call | tf_op jit(solution)/shard_map/pallas_call | solution.py:356
  52.2 0.6 %copy.9 = bf16[4,1024]{1,0:T(4,128)(2,1)} copy(bf16[4,1024]{1,0:T(4,128)(2,1)S(1)} %get-tuple-element.2) | data formatting | bytes 16384
  52.8 1.0 %copy.10 = f32[512,512]{1,0:T(8,128)} copy(f32[512,512]{1,0:T(8,128)S(1)} %get-tuple-element.3) | data formatting | bytes 2097152

commit v5 on v4

--- a/solution.py
+++ b/solution.py
@@ -11,7 +11,7 @@
 MSG = 384
 ZMSG = 640
 OFFSETS = (0, 1, -1, 2, -2, 3, -3, 4)
-SIDE = {1: (0, -1, 3), 2: (0, 1, 1), 5: (3, -1, 3), 6: (4, 1, 1)}
+SIDE = {1: (0, -1, 3), 2: (0, 1, 1)}
 BATCHES = ((0, 1), (1, 3), (3, 5), (5, 7), (7, 8))
 
 
@@ -245,7 +245,7 @@
 
     def along_b(k, i, back):
         lo, hi = BATCHES[k]
-        if lo % 4 == 1:
+        if lo == 1:
             lo, hi = (lo + 1, hi) if i == 1 else (lo, hi - 1)
         bb = (b + 4 - i) % 4 if back else b
         return copy(raw.at[c, lo:hi, bb], b_recv.at[k, i], at_plane(c, (b + i) % 4, a))
@@ -269,7 +269,7 @@
             along_a(k, i, False).start()
 
     def peers_of(k):
-        return (1, 3) if BATCHES[k][0] % 4 == 1 else (2, 1, 3)
+        return (1, 3) if BATCHES[k][0] == 1 else (2, 1, 3)
 
     def stage_a(k):
         for i in (1, 3, 2):
@@ -338,11 +338,11 @@
     stage_b(1)
     stage_b(2)
     stage_dot(1)
+    stage_b(3)
+    stage_dot(2)
     stage_b(4)
-    stage_dot(2)
-    stage_b(3)
+    stage_dot(3)
     stage_dot(4)
-    stage_dot(3)
 
     whole.wait_send()
     for move in across:

time: 53.9 us -> 53.5 us (level)
  no operation moved by 1% of the time
where the time goes in v5:
time: 53.5 us; the launch traced here: 53.3 us
  Pallas kernels  51.1 us (96%)
  local copies, waits for them, and re-layouts  1.57 us (3%)
  between operations  0.64 us (1%)
    pallas_call x1, Pallas kernels, shards(): pl.pallas_call(kernel, out_shape=(pltpu.VMEM((4, 1024), BF16), pltpu.VMEM...  51.1 us
    unnamed x2, local copies, waits for them, and re-layouts  1.57 us

profile of v5, /device:TPU:1, one launch (start us, length us, event | category | flops | bytes accessed | tf_op | source)
XLA Modules:
  0.0 53.3 jit_solution(10073898577197818529)
XLA Ops:
  0.6 51.1 %shard_map.68 = (bf16[4,1024]{1,0:T(4,128)(2,1)S(1)}, f32[512,512]{1,0:T(8,128)S(1)}) custom-call(bf16[512,1024]{1,0:T(8,128)(2,1)} %emb_hbm.1, s32[1,512]{1,0:T(1,128)} %bitcast.1, s32[1,64]{1,0:T(1,128)} %listing_hbm.1, s32[1,256]{1,0:T(1,128)} %owner_hbm.1, f32[4,1024]{1,0:T(4,128)} %old_hbm.1), custom_call_target="tpu_custom_call" | custom-call | tf_op jit(solution)/shard_map/pallas_call | solution.py:356
  51.8 0.6 %copy.9 = bf16[4,1024]{1,0:T(4,128)(2,1)} copy(bf16[4,1024]{1,0:T(4,128)(2,1)S(1)} %get-tuple-element.2) | data formatting | bytes 16384
  52.4 1.0 %copy.10 = f32[512,512]{1,0:T(8,128)} copy(f32[512,512]{1,0:T(8,128)S(1)} %get-tuple-element.3) | data formatting | bytes 2097152

commit v6 on v5

--- a/solution.py
+++ b/solution.py
@@ -294,12 +294,10 @@
     def one_group(n, carry):
         offset = jnp.where(n % 2 == 1, (n + 1) // 2, -(n // 2))
         gg = (z + offset + 20) % 8
-        first = raw[0, n].reshape(256, 512)
-        second = raw[1, n].reshape(256, 512)
+        both = jnp.concatenate([raw[0, n].reshape(256, 512), raw[1, n].reshape(256, 512)], axis=0)
         for h in range(2):
             rows = slice(256 * h, 256 * h + 256)
-            turned = jnp.dot(perm[rows, :256], first, preferred_element_type=F32)
-            turned = turned + jnp.dot(perm[rows, 256:], second, preferred_element_type=F32)
+            turned = jnp.dot(perm[rows, :], both, preferred_element_type=F32)
             slab[:, 512 * h:512 * h + 512] = turned.astype(BF16)
         lanes = pl.ds(pl.multiple_of((gg // 2) * 128, 128), 128)
         for r in range(0, 512, 256):

time: 53.5 us -> 53.5 us (level)
  no operation moved by 1% of the time
where the time goes in v6:
time: 53.5 us; the launch traced here: 53.3 us
  Pallas kernels  51.1 us (96%)
  local copies, waits for them, and re-layouts  1.57 us (3%)
  between operations  0.64 us (1%)
    pallas_call x1, Pallas kernels, shards(): pl.pallas_call(kernel, out_shape=(pltpu.VMEM((4, 1024), BF16), pltpu.VMEM...  51.1 us
    unnamed x2, local copies, waits for them, and re-layouts  1.57 us

profile of v6, /device:TPU:1, one launch (start us, length us, event | category | flops | bytes accessed | tf_op | source)
XLA Modules:
  0.0 53.3 jit_solution(24534186415436081)
XLA Ops:
  0.6 51.1 %shard_map.68 = (bf16[4,1024]{1,0:T(4,128)(2,1)S(1)}, f32[512,512]{1,0:T(8,128)S(1)}) custom-call(bf16[512,1024]{1,0:T(8,128)(2,1)} %emb_hbm.1, s32[1,512]{1,0:T(1,128)} %bitcast.1, s32[1,64]{1,0:T(1,128)} %listing_hbm.1, s32[1,256]{1,0:T(1,128)} %owner_hbm.1, f32[4,1024]{1,0:T(4,128)} %old_hbm.1), custom_call_target="tpu_custom_call" | custom-call | tf_op jit(solution)/shard_map/pallas_call | solution.py:354
  51.8 0.6 %copy.9 = bf16[4,1024]{1,0:T(4,128)(2,1)} copy(bf16[4,1024]{1,0:T(4,128)(2,1)S(1)} %get-tuple-element.2) | data formatting | bytes 16384
  52.4 1.0 %copy.10 = f32[512,512]{1,0:T(8,128)} copy(f32[512,512]{1,0:T(8,128)S(1)} %get-tuple-element.3) | data formatting | bytes 2097152
